TPU v7x, 256 devices: a whole 4x4x8 slice. The times are simulated.
256 devices in a mesh: vert: 128 (over z, y, x), qcol: 2 (over core).
Axes of the slice: x: 4, y: 4, z: 8, core: 2. Of those that a mesh axis runs over, the one named last changes fastest.
Arguments:
- descriptors: bfloat16 [262144, 2048], P('vert'), may hold values from -0.8984375 to 0.8984375
- queries: bfloat16 [512, 2048], P('qcol', 'vert'), may hold values from -0.8984375 to 0.8984375
- tiles: bfloat16 [6144, 128, 128], P('vert'), may hold values from 0 to 1, as said below
- tile_cols: int32 [128, 3, 16], replicated, may hold values from 0 to 15, as said below
- part_size: int32 [128], replicated, may hold values from 1024 to 2048, as said below
Outputs:
- ranking: float32 [262144, 512], P('vert', 'qcol')
- residual: float32 [262144, 512], P('vert', 'qcol')
Inputs may be any that keep to these rules, and one draw needn't show every extreme that they name: For each part d and slot j, tile_cols[d, j, :] is a permutation of 0 to 15. `part_size`: some part has exactly 2048 live vertices and some exactly 1024. tiles are sparse and nonnegative; every row and every column of B sums to at most 1.01.
All inputs are finite; a program needn't handle non-finite values.
Results may differ from a plain program's by a relative error of at most 0.0003.
Values may be sent and summed in bfloat16 or wider, within the bound.
A program may use at most 128 MiB of HBM per device.

v0:
```python
import jax
import jax.numpy as jnp
from jax import lax
from jax.sharding import PartitionSpec as P

ITERS = 2


def padded(block, sides, width):
    for axis, dim in sides:
        count = lax.axis_size(axis)
        forward = [(i, i + 1) for i in range(count - 1)]
        forward.append((count - 1, 0))
        backward = [(target, source) for source, target in forward]
        low = lax.ppermute(
            lax.slice_in_dim(block, block.shape[dim] - width, None, axis=dim), axis, forward
        )
        high = lax.ppermute(lax.slice_in_dim(block, 0, width, axis=dim), axis, backward)
        block = jnp.concatenate([low, block, high], axis=dim)
    return block


def shifted(x, axis, by):
    peers = lax.axis_size(axis)
    return lax.ppermute(x, axis, [(i, (i + by) % peers) for i in range(peers)])


def transposed(blocks_slot, rows3, cols_row):
    moved = jnp.einsum("rba,rbq->raq", blocks_slot, rows3, precision=lax.Precision.HIGHEST)
    return moved[jnp.argsort(cols_row)]


def body(descriptors, queries, tiles, tile_cols, part_size):
    rows = descriptors.shape[0]
    qdev = queries.shape[0]
    tile = tiles.shape[1]
    rtiles = rows // tile
    slots = tiles.shape[0] // rtiles
    here = lax.axis_index("vert")
    sims = lax.dot_general(
        descriptors,
        lax.all_gather(queries, "vert", axis=1, tiled=True),
        (((1,), (1,)), ((), ())),
        preferred_element_type=jnp.float32,
    )
    live_count = lax.dynamic_index_in_dim(part_size, here, 0, keepdims=False)
    live = (lax.iota(jnp.int32, rows) < live_count).astype(jnp.float32)[:, None]
    seeds = live * jnp.maximum(sims, 0.0) ** 3
    blocks = tiles.astype(jnp.float32).reshape(slots, rtiles, tile, tile)
    own_cols = lax.dynamic_index_in_dim(tile_cols, here, 0, keepdims=False)

    def squares(values):
        return lax.psum(jnp.sum(values * values, axis=0), "vert")

    ranking = jnp.zeros_like(seeds)
    residual = seeds
    direction = seeds
    norm_now = squares(residual)
    for step in range(ITERS):
        widened = padded(direction, (("vert", 0),), rows)
        forward = jnp.zeros((rtiles, tile, qdev), jnp.float32)
        for slot in range(slots):
            source = widened[slot * rows : (slot + 1) * rows].reshape(rtiles, tile, qdev)
            picked = source[own_cols[slot]]
            forward = forward + jnp.einsum(
                "rab,rbq->raq", blocks[slot], picked, precision=lax.Precision.HIGHEST
            )
        own3 = direction.reshape(rtiles, tile, qdev)
        middle = transposed(blocks[1], own3, own_cols[1])
        toward_low = transposed(blocks[0], own3, own_cols[0])
        toward_high = transposed(blocks[slots - 1], own3, own_cols[slots - 1])
        back = middle + shifted(toward_low, "vert", -1) + shifted(toward_high, "vert", 1)
        both = (forward + back).reshape(rows, qdev)
        image = direction - 0.99 * live * (0.5 * both)
        curve = lax.psum(jnp.sum(direction * image, axis=0), "vert")
        alpha = norm_now / curve
        ranking = ranking + alpha[None, :] * direction
        residual = residual - alpha[None, :] * image
        norm_next = squares(residual)
        direction = residual + (norm_next / norm_now)[None, :] * direction
        norm_now = norm_next
    return (ranking, residual)


def solution(mesh):
    placed = (P("vert", None), P("qcol", "vert"), P("vert", None, None), P(), P())
    return jax.shard_map(
        body,
        mesh=mesh,
        in_specs=placed,
        out_specs=(P("vert", "qcol"), P("vert", "qcol")),
        check_vma=False,
    )
```

profile of v0, /device:TPU:2, one launch (start us, length us, event | category | flops | bytes accessed | tf_op | source)
XLA Modules:
  0.0 1346.1 jit_solution(10652084589290533953)
XLA Ops:
  14.6 102.0 %all-gather.2.cloned.1.call-done = bf16[256,2048]{0,1:T(8,128)(2,1)} async-done(((bf16[256,16]{0,1:T(8,128)(2,1)}), bf16[256,2048]{0,1:T(8,128)(2,1)}) %all-gather.2.cloned.1.call-update) | async-done | bytes 1048592 | tf_op jit(solution)/shard_map/all_gather | solution.py:42
  116.7 6.1 fusion
  124.9 4.3 convolution_bitcast_fusion.4
  132.1 3.6 gather_fusion.4
  135.7 6.1 collective-permute-start.2
  141.8 4.3 convolution_bitcast_fusion.3
  149.0 3.6 gather_fusion.5
  153.3 4.3 convolution_bitcast_fusion.5
  162.6 3.6 gather_fusion.3
  166.1 4.1 fusion.17
  171.5 3.6 gather_fusion
  175.2 3.7 gather_fusion.2
  181.8 30.5 %collective-permute-done.2 = f32[16,128,256]{2,1,0:T(8,128)} collective-permute-done((f32[16,128,256]{2,1,0:T(8,128)}, f32[16,128,256]{2,1,0:T(8,128)}, u32[]{:S(2)}, u32[]{:S(2)}) %collective-permute-start.2) | collective-permute-done | bytes 2097184 | tf_op jit(solution)/shard_map/ppermute | solution.py:25
  212.3 5.1 bitcast_add_fusion.1
  218.8 347.2 %all-reduce = (f32[256]{0:T(256)S(1)}, f32[256]{0:T(256)S(1)}) all-reduce(f32[256]{0:T(256)S(1)} %get-tuple-element.9, f32[256]{0:T(256)S(1)} %get-tuple-element.8), channel_id=1, replica_groups=mesh['vert'=128,'qcol'=2] {'vert'}, use_global_device_ids=true, to_apply=%region_1.2 | all-reduce | flops 512 | bytes 4096 | tf_op jit(solution)/shard_map/psum | solution.py:53
  568.1 350.2 %psum.30 = f32[256]{0:T(256)S(1)} all-reduce(f32[256]{0:T(256)S(1)} %multiply_reduce_fusion.1), channel_id=1, replica_groups=mesh['vert'=128,'qcol'=2] {'vert'}, use_global_device_ids=true, to_apply=%region_8.9 | all-reduce | flops 256 | bytes 2048 | tf_op jit(solution)/shard_map/psum | solution.py:53
  918.4 3.4 multiply_add_fusion.1
  923.8 4.9 convolution_bitcast_fusion.1
  931.6 3.6 gather_fusion.10
  935.2 5.5 collective-permute-start.6
  940.7 4.9 convolution_bitcast_fusion
  948.6 3.6 gather_fusion.11
  952.2 3.6 gather_fusion.7
  955.8 5.0 convolution_bitcast_fusion.2
  963.7 3.6 gather_fusion.9
  967.4 4.1 fusion.14
  971.5 3.6 gather_fusion.6
  975.1 3.6 gather_fusion.8
  978.7 3.0 fusion.20
  981.8 5.1 bitcast_add_fusion
  990.1 344.6 %psum.31 = f32[256]{0:T(256)S(1)} all-reduce(f32[256]{0:T(256)S(1)} %multiply_reduce_fusion), channel_id=1, replica_groups=mesh['vert'=128,'qcol'=2] {'vert'}, use_global_device_ids=true, to_apply=%region_10.11 | all-reduce | flops 256 | bytes 2048 | tf_op jit(solution)/shard_map/psum | solution.py:75
  1334.7 4.6 multiply_subtract_fusion
  (62 shorter events, 42.7 us)
Async XLA Ops:
  7.2 109.5 %all-gather.2.cloned.1.call-start = ((), (), s32[]{:S(2)}) async-start(), calls=%async_computation | async-start | bytes 1056768 | tf_op jit(solution)/shard_map/all_gather | solution.py:42
  122.8 48.8 %collective-permute-start = (f32[2048,256]{1,0:T(8,128)S(1)}, f32[2048,256]{1,0:T(8,128)}, u32[]{:S(2)}, u32[]{:S(2)}) collective-permute-start(f32[2048,256]{1,0:T(8,128)S(1)} %fusion), channel_id=1, source_target_pairs={{0,2},{2,4},{4,6},{6,8},{8,10},{10,12},{12,14},{14,16},{16,18},{18... | collective-permute-start | bytes 6291464 | tf_op jit(solution)/shard_map/ppermute | solution.py:15
  124.5 50.7 %collective-permute-start.1 = (f32[2048,256]{1,0:T(8,128)S(1)}, f32[2048,256]{1,0:T(8,128)}, u32[]{:S(2)}, u32[]{:S(2)}) collective-permute-start(f32[2048,256]{1,0:T(8,128)S(1)} %fusion), channel_id=1, source_target_pairs={{2,0},{4,2},{6,4},{8,6},{10,8},{12,10},{14,12},{16,14},{18,16},{20... | collective-permute-start | bytes 6291464 | tf_op jit(solution)/shard_map/ppermute | solution.py:18
  135.7 76.6 %collective-permute-start.2 = (f32[16,128,256]{2,1,0:T(8,128)}, f32[16,128,256]{2,1,0:T(8,128)}, u32[]{:S(2)}, u32[]{:S(2)}) collective-permute-start(f32[16,128,256]{2,1,0:T(8,128)} %gather_fusion.4), channel_id=1, source_target_pairs={{0,254},{2,0},{4,2},{6,4},{8,6},{10,8},{12,10},{14,12},{16,14},{18... | collective-permute-start | bytes 6291464 | tf_op jit(solution)/shard_map/ppermute | solution.py:25
  152.6 59.7 %collective-permute-start.3 = (f32[16,128,256]{2,1,0:T(8,128)}, f32[16,128,256]{2,1,0:T(8,128)}, u32[]{:S(2)}, u32[]{:S(2)}) collective-permute-start(f32[16,128,256]{2,1,0:T(8,128)} %gather_fusion.5), channel_id=1, source_target_pairs={{0,2},{2,4},{4,6},{6,8},{8,10},{10,12},{12,14},{14,16},{16,18},{18... | collective-permute-start | bytes 6291464 | tf_op jit(solution)/shard_map/ppermute | solution.py:25
  178.8 33.5 %copy-start.4 = (f32[16,128,256]{2,1,0:T(8,128)S(1)}, f32[16,128,256]{2,1,0:T(8,128)}, u32[]{:S(2)}) copy-start(f32[16,128,256]{2,1,0:T(8,128)} %gather_fusion.3) | copy-start | bytes 6291460
  178.8 33.5 %copy-start.5 = (f32[16,256,128]{1,2,0:T(8,128)S(1)}, f32[16,256,128]{1,2,0:T(8,128)}, u32[]{:S(2)}) copy-start(f32[16,256,128]{1,2,0:T(8,128)} %fusion.17) | copy-start | bytes 6291460
  217.5 1.4 copy-start
  921.8 49.7 %collective-permute-start.4 = (f32[2048,256]{1,0:T(8,128)}, f32[2048,256]{1,0:T(8,128)}, u32[]{:S(2)}, u32[]{:S(2)}) collective-permute-start(f32[2048,256]{1,0:T(8,128)} %multiply_add_fusion.1), channel_id=1, source_target_pairs={{0,2},{2,4},{4,6},{6,8},{8,10},{10,12},{12,14},{14,16},{16,18},{18... | collective-permute-start | bytes 6291464 | tf_op jit(solution)/shard_map/ppermute | solution.py:15
  921.8 53.4 %collective-permute-start.5 = (f32[2048,256]{1,0:T(8,128)}, f32[2048,256]{1,0:T(8,128)}, u32[]{:S(2)}, u32[]{:S(2)}) collective-permute-start(f32[2048,256]{1,0:T(8,128)} %multiply_add_fusion.1), channel_id=1, source_target_pairs={{2,0},{4,2},{6,4},{8,6},{10,8},{12,10},{14,12},{16,14},{18,16},{20... | collective-permute-start | bytes 6291464 | tf_op jit(solution)/shard_map/ppermute | solution.py:18
  935.2 46.5 %collective-permute-start.6 = (f32[16,128,256]{2,1,0:T(8,128)}, f32[16,128,256]{2,1,0:T(8,128)}, u32[]{:S(2)}, u32[]{:S(2)}) collective-permute-start(f32[16,128,256]{2,1,0:T(8,128)} %gather_fusion.10), channel_id=1, source_target_pairs={{0,254},{2,0},{4,2},{6,4},{8,6},{10,8},{12,10},{14,12},{16,14},{18... | collective-permute-start | bytes 6291464 | tf_op jit(solution)/shard_map/ppermute | solution.py:25
  952.2 29.5 %collective-permute-start.7 = (f32[16,128,256]{2,1,0:T(8,128)}, f32[16,128,256]{2,1,0:T(8,128)}, u32[]{:S(2)}, u32[]{:S(2)}) collective-permute-start(f32[16,128,256]{2,1,0:T(8,128)} %gather_fusion.11), channel_id=1, source_target_pairs={{0,2},{2,4},{4,6},{6,8},{8,10},{10,12},{12,14},{14,16},{16,18},{18... | collective-permute-start | bytes 6291464 | tf_op jit(solution)/shard_map/ppermute | solution.py:25
  978.7 3.0 copy-start.2
  978.7 3.0 copy-start.3
  986.9 1.3 copy-start.1
Sparse Core Ops, SparseCore 0:
  11.4 105.2 all-gather.1
where the time goes:
time: 1350 us
  blocking collectives  1040 us (77%)
  waiting for transfers between devices  134 us (10%)
  local copies, waits for them, and re-layouts  63.5 us (5%)
  matrix products  58.5 us (4%)
  other arithmetic  17.7 us (1%)
  starting transfers between devices  15.8 us (1%)
  between operations  14.2 us (1%)
    psum x2, blocking collectives, squares(): return lax.psum(jnp.sum(values * values, axis=0), 'vert')  697 us
    psum x1, blocking collectives, body(): curve = lax.psum(jnp.sum(direction * image, axis=0), 'vert')  345 us
    all_gather x1, waiting for transfers between devices, body(): lax.all_gather(queries, 'vert', axis=1, tiled=True)  102 us
    ppermute x4, waiting for transfers between devices, shifted(): return lax.ppermute(x, axis, [(i, (i + by) % peers) for i in range(peers)])  30.5 us
    dot_general x6, matrix products, transposed(): jnp.einsum('rba,rbq->raq', blocks_slot, rows3, precision=lax.Precision.HI...  27.8 us
  transfers between devices with their start and end apart: 9, of which 3 were waited for; matrix products, arithmetic and copies ran while one was open for 8% of the time, Pallas kernels for 0%

commit v1 on v0

v1 whole, which is shorter than its diff:
```python
import functools

import jax
import jax.numpy as jnp
from jax import lax
from jax.experimental import pallas as pl
from jax.experimental.pallas import tpu as pltpu
from jax.sharding import PartitionSpec as P

XS, YS = 4, 4
LANES = 128
STEPS = 65535.0
DAMP = 0.99
MESH = pl.DeviceIdType.MESH
F32, BF16, I32 = jnp.float32, jnp.bfloat16, jnp.int32


def kernel(
    n, desc_ref, q_ref, tiles_ref, cols_ref, size_ref,
    s0_ref, m0_ref, m1_ref, coef_ref,
    desc_v, tiles_v, nbr_tiles, w_v, qg, qcat, code_v, halo_v, scale_v, hscale_v, own_hl, halo_hl, red_v,
    cols_s, inv_s, local_sem, send_sem, recv_sem,
):
    zs = n // (XS * YS)
    rows = desc_ref.shape[0]
    rt = rows // LANES
    qdev = q_ref.shape[0]
    halves = qdev // LANES
    me = lax.axis_index("vert")
    x = lax.rem(me, XS)
    y = lax.rem(lax.div(me, XS), YS)
    z = lax.div(me, XS * YS)
    right, left = lax.rem(me + 1, n), lax.rem(me + n - 1, n)
    sizes = (XS, YS, zs)
    place = (x, y, z)

    def peer(axis, k):
        if axis == 0:
            return me - x + lax.rem(x + k, XS)
        if axis == 1:
            return me + (lax.rem(y + k, YS) - y) * XS
        return lax.rem(me + k * (XS * YS), n)

    used = [0]
    sent = []

    def send(src, dst, target):
        i = used[0]
        used[0] += 1
        copy = pltpu.make_async_remote_copy(
            src_ref=src, dst_ref=dst, send_sem=send_sem.at[i], recv_sem=recv_sem.at[i],
            device_id={"vert": target}, device_id_type=MESH,
        )
        copy.start()
        sent.append(copy)
        return copy

    partners = [peer(a, k) for a in range(3) for k in range(1, sizes[a])] + [right, left]
    barrier = pltpu.get_barrier_semaphore()
    for p in partners:
        pl.semaphore_signal(barrier, inc=1, device_id={"vert": p}, device_id_type=MESH)

    fetch_desc = pltpu.make_async_copy(desc_ref, desc_v, local_sem.at[0])
    fetch_desc.start()
    fetch_tiles = pltpu.make_async_copy(tiles_ref, tiles_v, local_sem.at[1])
    fetch_tiles.start()
    fetch_cols = []
    for i in range(3):
        part = lax.rem(me + n + i - 1, n)
        fetch_cols.append(pltpu.make_async_copy(cols_ref.at[part], cols_s.at[i], local_sem.at[2 + i]))
        fetch_cols[-1].start()

    block = q_ref.shape[1]
    eye = (lax.broadcasted_iota(I32, (block, block), 0) == lax.broadcasted_iota(I32, (block, block), 1)).astype(BF16)
    turned = lax.dot_general(eye, q_ref[...], (((1,), (1,)), ((), ())), preferred_element_type=F32).astype(BF16)
    for h in range(halves):
        qg[h, z, y, x] = turned[:, h * LANES : (h + 1) * LANES]
    live_count = size_ref[me]

    pl.semaphore_wait(barrier, len(partners))

    step1 = [send(qg.at[:, z, y, x], qg.at[:, z, y, x], peer(2, k)) for k in range(1, zs)]
    for c in step1:
        c.wait_recv()
    step2a = [send(qg.at[0, :, y, x], qg.at[0, :, y, x], peer(1, k)) for k in range(1, YS)]
    step2b = [send(qg.at[1, :, y, x], qg.at[1, :, y, x], peer(0, k)) for k in range(1, XS)]
    for c in step2a:
        c.wait_recv()
    step3a = [send(qg.at[0, :, :, x], qg.at[0, :, :, x], peer(0, k)) for k in range(1, XS)]
    for c in step2b:
        c.wait_recv()
    step3b = [send(qg.at[1, :, y], qg.at[1, :, y], peer(1, k)) for k in range(1, YS)]

    to_left = send(tiles_ref.at[pl.ds(0, rt)], nbr_tiles.at[1], left)
    to_right = send(tiles_ref.at[pl.ds(2 * rt, rt)], nbr_tiles.at[0], right)

    for c in fetch_cols:
        c.wait()
    for i in range(3):
        def invert(r, _, i=i):
            found = jnp.int32(0)
            for t in range(rt):
                found = jnp.where(cols_s[i, 2 - i, t] == r, jnp.int32(t), found)
            inv_s[i, r] = found
            return 0

        lax.fori_loop(0, rt, invert, 0)

    fetch_tiles.wait()

    def ours(r, _):
        for i in range(3):
            w_v[i, r, :, :LANES] = tiles_v[i * rt + r]
        w_v[1, r, :, LANES:] = tiles_v[rt + inv_s[1, r]].T
        return 0

    lax.fori_loop(0, rt, ours, 0)

    def gathered(h, copies):
        for c in copies:
            c.wait_recv()
        qcat[:, h * LANES : (h + 1) * LANES] = qg[h].reshape(qcat.shape[0], LANES)

    gathered(0, step3a)
    gathered(1, step3b)
    fetch_desc.wait()

    chunk = min(512, rows)

    def fold(values):
        return values.reshape(values.shape[0] // 8, 8, values.shape[1])

    def live_of(start, shape):
        return lax.broadcasted_iota(I32, shape, 0) + start < live_count

    def seed(i, carry):
        most, square = carry
        at = pl.ds(pl.multiple_of(i * chunk, chunk), chunk)
        sims = jnp.dot(desc_v[at, :], qcat[...], preferred_element_type=F32)
        pos = jnp.maximum(sims, 0.0)
        s = jnp.where(live_of(i * chunk, sims.shape), pos * pos * pos, 0.0)
        s0_ref[at, :] = s
        return jnp.maximum(most, jnp.max(fold(s), axis=0)), square + jnp.sum(fold(s * s), axis=0)

    zero = jnp.zeros((8, qdev), F32)
    most, square0 = lax.fori_loop(0, rows // chunk, seed, (zero, zero))

    def encode(it, h, src_ref, most):
        cut = slice(h * LANES, (h + 1) * LANES)
        top = jnp.max(most, axis=0, keepdims=True)
        ok = top > 1e-30
        inverse = jnp.where(ok, STEPS / jnp.where(ok, top, 1.0), 0.0)
        scale_v[it, h] = jnp.broadcast_to(top * (1.0 / STEPS), (8, LANES))

        def one(r, _):
            at = pl.ds(pl.multiple_of(r * LANES, LANES), LANES)
            v = src_ref[at, cut]
            code_v[it, h, r] = ((v * inverse + 0.5).astype(I32) - 32768).astype(jnp.int16)
            hi = v.astype(BF16)
            own_hl[h, r, :, :LANES] = hi
            own_hl[h, r, :, LANES:] = (v - hi.astype(F32)).astype(BF16)
            return 0

        lax.fori_loop(0, rt, one, 0)
        copies = []
        for side, target in ((1, left), (0, right)):
            copies.append(send(scale_v.at[it, h], hscale_v.at[it, h, side], target))
            copies.append(send(code_v.at[it, h], halo_v.at[it, h, side], target))
        return copies

    def decode(it, h, copies):
        for c in copies:
            c.wait_recv()
        for side in range(2):
            def one(r, _, side=side):
                v = halo_v[it, h, side, r].astype(I32) + 32768
                halo_hl[side, r, :, :LANES] = lax.shift_right_logical(v, 8).astype(F32).astype(BF16)
                halo_hl[side, r, :, LANES:] = lax.bitwise_and(v, 255).astype(F32).astype(BF16)
                return 0

            lax.fori_loop(0, rt, one, 0)

    def apply(it, h, out_ref, use, carry):
        cut = slice(h * LANES, (h + 1) * LANES)
        low, high = hscale_v[it, h, 0][:1], hscale_v[it, h, 1][:1]

        def one(r, carry):
            at = pl.ds(pl.multiple_of(r * LANES, LANES), LANES)
            from_left = jnp.dot(
                w_v[0, r],
                jnp.concatenate([halo_hl[0, cols_s[1, 0, r]], halo_hl[0, inv_s[0, r]]], axis=0),
                preferred_element_type=F32,
            )
            from_own = jnp.dot(
                w_v[1, r],
                jnp.concatenate([own_hl[h, cols_s[1, 1, r]], own_hl[h, inv_s[1, r]]], axis=0),
                preferred_element_type=F32,
            )
            from_right = jnp.dot(
                w_v[2, r],
                jnp.concatenate([halo_hl[1, cols_s[1, 2, r]], halo_hl[1, inv_s[2, r]]], axis=0),
                preferred_element_type=F32,
            )
            total = (from_left[:, :LANES] * 256.0 + from_left[:, LANES:]) * low
            total = total + (from_own[:, :LANES] + from_own[:, LANES:])
            total = total + (from_right[:, :LANES] * 256.0 + from_right[:, LANES:]) * high
            m = jnp.where(live_of(r * LANES, total.shape), 0.5 * total, 0.0)
            out_ref[at, cut] = m
            return use(carry, at, cut, m)

        return lax.fori_loop(0, rt, one, carry)

    def total_of(p, first, second):
        row = lax.broadcasted_iota(I32, (8, qdev), 0)
        value = jnp.where(
            row == 0,
            jnp.sum(first, axis=0, keepdims=True),
            jnp.where(row == 1, jnp.sum(second, axis=0, keepdims=True), 0.0),
        )
        base = 0
        for axis in range(3):
            mine = base + place[axis]
            red_v[p, mine] = value
            copies = [send(red_v.at[p, mine], red_v.at[p, mine], peer(axis, k)) for k in range(1, sizes[axis])]
            for c in copies:
                c.wait_recv()
            value = red_v[p, base]
            for k in range(1, sizes[axis]):
                value = value + red_v[p, base + k]
            base += sizes[axis]
        return value[0:1], value[1:2]

    halo0 = [encode(0, h, s0_ref, most[:, h * LANES : (h + 1) * LANES]) for h in range(halves)]

    for side, copy in ((1, to_left), (0, to_right)):
        copy.wait_recv()

    def theirs(r, _):
        w_v[0, r, :, LANES:] = nbr_tiles[0, inv_s[0, r]].T
        w_v[2, r, :, LANES:] = nbr_tiles[1, inv_s[2, r]].T
        return 0

    lax.fori_loop(0, rt, theirs, 0)

    def first_use(carry, at, cut, m):
        most, curve = carry
        s0 = s0_ref[at, cut]
        return jnp.maximum(most, jnp.max(fold(m), axis=0)), curve + jnp.sum(fold(s0 * (s0 - DAMP * m)), axis=0)

    small = jnp.zeros((8, LANES), F32)
    halo1, curves = [], []
    for h in range(halves):
        decode(0, h, halo0[h])
        most, curve = apply(0, h, m0_ref, first_use, (small, small))
        curves.append(curve)
        halo1.append(encode(1, h, m0_ref, most))

    rr0, curve0 = total_of(0, square0, jnp.concatenate(curves, axis=1))
    alpha0 = rr0 / curve0

    def residual_square(r, square):
        at = pl.ds(pl.multiple_of(r * LANES, LANES), LANES)
        s0 = s0_ref[at, :]
        r1 = s0 - alpha0 * (s0 - DAMP * m0_ref[at, :])
        return square + jnp.sum(fold(r1 * r1), axis=0)

    square1 = lax.fori_loop(0, rt, residual_square, zero)
    rr1, _ = total_of(1, square1, square1)
    beta = rr1 / rr0

    def second_use(curve, at, cut, m1):
        s0, m0 = s0_ref[at, cut], m0_ref[at, cut]
        a, b = alpha0[:, cut], beta[:, cut]
        d1 = (s0 - a * (s0 - DAMP * m0)) + b * s0
        image = d1 - DAMP * ((1.0 + b) * m0 - a * (m0 - DAMP * m1))
        return curve + jnp.sum(fold(d1 * image), axis=0)

    curves = []
    for h in range(halves):
        decode(1, h, halo1[h])
        curves.append(apply(1, h, m1_ref, second_use, small))
    curve = jnp.concatenate(curves, axis=1)
    curve1, _ = total_of(2, curve, curve)
    alpha1 = rr1 / curve1
    row = lax.broadcasted_iota(I32, (8, qdev), 0)
    coef_ref[...] = jnp.where(row == 0, alpha0, jnp.where(row == 1, beta, alpha1))

    for c in sent:
        c.wait_send()


def body(descriptors, queries, tiles, tile_cols, part_size):
    n = lax.axis_size("vert")
    rows, width = descriptors.shape
    qdev, block = queries.shape
    rt = rows // LANES
    halves = qdev // LANES
    zs = n // (XS * YS)
    field = pltpu.VMEM((rows, qdev), F32)
    hops = XS + YS + zs - 3
    copies = (zs - 1 + 2 * (XS + YS - 2)) + 2 + 2 * halves * 4 + 3 * hops
    s0, m0, m1, coef = pl.pallas_call(
        functools.partial(kernel, n),
        out_shape=(field, field, field, pltpu.VMEM((8, qdev), F32)),
        in_specs=[
            pl.BlockSpec(memory_space=pl.ANY),
            pl.BlockSpec(memory_space=pltpu.VMEM),
            pl.BlockSpec(memory_space=pl.ANY),
            pl.BlockSpec(memory_space=pl.ANY),
            pl.BlockSpec(memory_space=pltpu.SMEM),
        ],
        out_specs=[pl.BlockSpec(memory_space=pltpu.VMEM)] * 4,
        scratch_shapes=[
            pltpu.VMEM((rows, width), BF16),
            pltpu.VMEM((3 * rt, LANES, LANES), BF16),
            pltpu.VMEM((2, rt, LANES, LANES), BF16),
            pltpu.VMEM((3, rt, LANES, 2 * LANES), BF16),
            pltpu.VMEM((halves, zs, YS, XS, block, LANES), BF16),
            pltpu.VMEM((width, qdev), BF16),
            pltpu.VMEM((2, halves, rt, LANES, LANES), jnp.int16),
            pltpu.VMEM((2, halves, 2, rt, LANES, LANES), jnp.int16),
            pltpu.VMEM((2, halves, 8, LANES), F32),
            pltpu.VMEM((2, halves, 2, 8, LANES), F32),
            pltpu.VMEM((halves, rt, LANES, 2 * LANES), BF16),
            pltpu.VMEM((2, rt, LANES, 2 * LANES), BF16),
            pltpu.VMEM((3, XS + YS + zs, 8, qdev), F32),
            pltpu.SMEM((3, 3, rt), I32),
            pltpu.SMEM((3, rt), I32),
            pltpu.SemaphoreType.DMA((5,)),
            pltpu.SemaphoreType.DMA((copies,)),
            pltpu.SemaphoreType.DMA((copies,)),
        ],
        compiler_params=pltpu.CompilerParams(
            collective_id=0, has_side_effects=True, vmem_limit_bytes=40 * 2**20
        ),
    )(descriptors, queries, tiles, tile_cols, part_size)
    alpha0, beta, alpha1 = coef[0:1], coef[1:2], coef[2:3]
    r1 = s0 - alpha0 * (s0 - DAMP * m0)
    d1 = r1 + beta * s0
    image = d1 - DAMP * ((1.0 + beta) * m0 - alpha0 * (m0 - DAMP * m1))
    return alpha0 * s0 + alpha1 * d1, r1 - alpha1 * image


def solution(mesh):
    placed = (P("vert", None), P("qcol", "vert"), P("vert", None, None), P(), P())
    return jax.shard_map(
        body,
        mesh=mesh,
        in_specs=placed,
        out_specs=(P("vert", "qcol"), P("vert", "qcol")),
        check_vma=False,
    )
```

time: 1350 us -> 160 us (0.12)
  blocking collectives: 1040 us -> 0 us
  Pallas kernels: 0 us -> 152 us
  waiting for transfers between devices: 134 us -> 0 us
  local copies, waits for them, and re-layouts: 63.5 us -> 3.76 us
  matrix products: 58.5 us -> 0 us
  starting transfers between devices: 15.8 us -> 0 us
  other arithmetic: 17.7 us -> 3.24 us
  between operations: 14.2 us -> 0.66 us
    psum x3 -> x0, blocking collectives: 1040 us -> none  [the longest x2 697 us: squares(): return lax.psum(jnp.sum(values * values, axis=0), 'vert')]
    pallas_call x0 -> x1, Pallas kernels: none -> 152 us  [body(): pl.pallas_call(functools.partial(kernel, n), out_shape=(field, field, fie...]
    all_gather x1 -> x0, waiting for transfers between devices: 102 us -> none  [body(): lax.all_gather(queries, 'vert', axis=1, tiled=True)]
    dot_general x13 -> x0, matrix products: 58.5 us -> none  [the longest x6 27.8 us: transposed(): jnp.einsum('rba,rbq->raq', blocks_slot, rows3, precision=lax.Precision.HI...]
    gather x12 -> x0, local copies, waits for them, and re-layouts: 41.7 us -> none  [the longest x6 21.6 us: transposed(): return moved[jnp.argsort(cols_row)]]
    ppermute x8 -> x0, waiting for transfers between devices: 31.8 us -> none  [the longest x4 30.5 us: shifted(): return lax.ppermute(x, axis, [(i, (i + by) % peers) for i in range(peers)])]
    dot_general x6 -> x0, local copies, waits for them, and re-layouts: 17.4 us -> none  [transposed(): jnp.einsum('rba,rbq->raq', blocks_slot, rows3, precision=lax.Precision.HI...]
    ppermute x8 -> x0, starting transfers between devices: 15.7 us -> none  [the longest x4 11.6 us: shifted(): return lax.ppermute(x, axis, [(i, (i + by) % peers) for i in range(peers)])]
  transfers between devices with their start and end apart: 9 -> 0, of which waited for: 3 -> 0; matrix products, arithmetic and copies ran while one was open for 8% -> 0% of each run, Pallas kernels for 0% -> 0%
where the time goes in v1:
time: 160 us; the launch traced here: 159 us
  Pallas kernels  152 us (95%)
  local copies, waits for them, and re-layouts  3.76 us (2%)
  other arithmetic  3.24 us (2%)
    pallas_call x1, Pallas kernels, body(): pl.pallas_call(functools.partial(kernel, n), out_shape=(field, field, fie...  152 us
    unnamed x6, local copies, waits for them, and re-layouts  3.76 us
    sub x1, other arithmetic, body(): return (alpha0 * s0 + alpha1 * d1, r1 - alpha1 * image)  3.23 us

profile of v1, /device:TPU:2, one launch (start us, length us, event | category | flops | bytes accessed | tf_op | source)
XLA Modules:
  0.0 159.2 jit_solution(7885182043939638362)
XLA Ops:
  0.6 0.8 copy.7.q_ref
  1.4 0.9 copy.8.cols_ref
  2.3 0.0 copy-start
  2.3 1.4 copy-done
  3.7 0.0 copy-start.1
  3.7 0.7 copy-done.1
  4.4 151.6 %shard_map.68 = (f32[2048,256]{1,0:T(8,128)S(1)}, f32[2048,256]{1,0:T(8,128)S(1)}, f32[2048,256]{1,0:T(8,128)S(1)}, f32[8,256]{1,0:T(8,128)S(1)}) custom-call(bf16[2048,2048]{1,0:T(8,128)(2,1)} %desc_ref.1, bf16[256,16]{1,0:T(8,128)(2,1)S(1)} %copy.7.q_ref, bf16[48,128,128]{2,1,0:T(8,128)(2,1)S(1)} %copy-done, s32[128,3,16]{2,1,0:T(4,128)S(1)} %copy.8.cols_ref, ...), custom_call_target="tpu_custom_call" | custom-call | tf_op jit(solution)/shard_map/pallas_call | solution.py:302
  156.0 3.2 %multiply_subtract_fusion = (f32[2048,256]{1,0:T(8,128)}, f32[2048,256]{1,0:T(8,128)}) fusion(f32[2048,256]{1,0:T(8,128)S(1)} %get-tuple-element.8, f32[2048,256]{1,0:T(8,128)S(1)} %get-tuple-element.9, f32[2048,256]{1,0:T(8,128)S(1)} %get-tuple-element.7, f32[256]{0:T(256)S(1)} %bitcast.4, f32[256]{0:T(256)S(1)} %bitcast.5, f32[256]{0:T(256)S(1)} %bitcast.6, ...), kind=kLoop, calls=%fused_computation | loop fusion | flops 9437184 | bytes 10489856 | tf_op jit(solution)/shard_map/sub | solution.py:341
  (1 shorter events, 0.0 us)
Async XLA Ops:
  2.3 1.4 copy-start
  3.7 0.7 copy-start.1

commit v2 on v1

--- a/solution.py
+++ b/solution.py
@@ -19,12 +19,12 @@
     n, desc_ref, q_ref, tiles_ref, cols_ref, size_ref,
     s0_ref, m0_ref, m1_ref, coef_ref,
     desc_v, tiles_v, nbr_tiles, w_v, qg, qcat, code_v, halo_v, scale_v, hscale_v, own_hl, halo_hl, red_v,
-    cols_s, inv_s, local_sem, send_sem, recv_sem,
+    cols_s, size_s, inv_s, local_sem, send_sem, recv_sem,
 ):
     zs = n // (XS * YS)
     rows = desc_ref.shape[0]
     rt = rows // LANES
-    qdev = q_ref.shape[0]
+    qdev = q_ref.shape[1]
     halves = qdev // LANES
     me = lax.axis_index("vert")
     x = lax.rem(me, XS)
@@ -32,7 +32,9 @@
     z = lax.div(me, XS * YS)
     right, left = lax.rem(me + 1, n), lax.rem(me + n - 1, n)
     sizes = (XS, YS, zs)
-    place = (x, y, z)
+    core, cores = lax.axis_index("qcol"), lax.axis_size("qcol")
+    plane = XS * YS
+    spot = lax.rem(me, plane)
 
     def peer(axis, k):
         if axis == 0:
@@ -49,34 +51,61 @@
         used[0] += 1
         copy = pltpu.make_async_remote_copy(
             src_ref=src, dst_ref=dst, send_sem=send_sem.at[i], recv_sem=recv_sem.at[i],
-            device_id={"vert": target}, device_id_type=MESH,
+            device_id=target if isinstance(target, dict) else {"vert": target}, device_id_type=MESH,
         )
         copy.start()
         sent.append(copy)
         return copy
 
-    partners = [peer(a, k) for a in range(3) for k in range(1, sizes[a])] + [right, left]
+    in_plane = [me - spot + lax.rem(y + j, YS) * XS + lax.rem(x + i, XS) for j in range(YS) for i in range(XS) if i or j]
+    along_z = [peer(2, k) for k in range(1, zs)]
+    others = [{"qcol": lax.rem(core + k, cores)} for k in range(1, cores)]
+    partners = [{"vert": p} for p in in_plane + along_z + [right, left]] + others
     barrier = pltpu.get_barrier_semaphore()
     for p in partners:
-        pl.semaphore_signal(barrier, inc=1, device_id={"vert": p}, device_id_type=MESH)
+        pl.semaphore_signal(barrier, inc=1, device_id=p, device_id_type=MESH)
 
     fetch_desc = pltpu.make_async_copy(desc_ref, desc_v, local_sem.at[0])
     fetch_desc.start()
     fetch_tiles = pltpu.make_async_copy(tiles_ref, tiles_v, local_sem.at[1])
     fetch_tiles.start()
-    fetch_cols = []
+    fetch_cols = pltpu.make_async_copy(cols_ref, cols_s, local_sem.at[2])
+    fetch_cols.start()
+    fetch_size = pltpu.make_async_copy(size_ref, size_s, local_sem.at[3])
+    fetch_size.start()
+    fetch_q = [
+        pltpu.make_async_copy(q_ref.at[:, h * LANES : (h + 1) * LANES], qg.at[h, z, y, x], local_sem.at[4 + h])
+        for h in range(halves)
+    ]
+    for c in fetch_q:
+        c.start()
+
+    fetch_cols.wait()
+    fetch_size.wait()
+    live_count = size_s[me]
+    parts = (left, me, right)
     for i in range(3):
-        part = lax.rem(me + n + i - 1, n)
-        fetch_cols.append(pltpu.make_async_copy(cols_ref.at[part], cols_s.at[i], local_sem.at[2 + i]))
-        fetch_cols[-1].start()
-
-    block = q_ref.shape[1]
-    eye = (lax.broadcasted_iota(I32, (block, block), 0) == lax.broadcasted_iota(I32, (block, block), 1)).astype(BF16)
-    turned = lax.dot_general(eye, q_ref[...], (((1,), (1,)), ((), ())), preferred_element_type=F32).astype(BF16)
-    for h in range(halves):
-        qg[h, z, y, x] = turned[:, h * LANES : (h + 1) * LANES]
-    live_count = size_ref[me]
-
+        def invert(r, _, i=i):
+            found = jnp.int32(0)
+            for t in range(rt):
+                found = jnp.where(cols_s[2 - i, t, parts[i]] == r, jnp.int32(t), found)
+            inv_s[i, r] = found
+            return 0
+
+        lax.fori_loop(0, rt, invert, 0)
+
+    fetch_tiles.wait()
+
+    def ours(r, _):
+        for i in range(3):
+            w_v[i, r, :, :LANES] = tiles_v[i * rt + r]
+        w_v[1, r, :, LANES:] = tiles_v[rt + inv_s[1, r]].T
+        return 0
+
+    lax.fori_loop(0, rt, ours, 0)
+
+    for c in fetch_q:
+        c.wait()
     pl.semaphore_wait(barrier, len(partners))
 
     step1 = [send(qg.at[:, z, y, x], qg.at[:, z, y, x], peer(2, k)) for k in range(1, zs)]
@@ -91,31 +120,6 @@
         c.wait_recv()
     step3b = [send(qg.at[1, :, y], qg.at[1, :, y], peer(1, k)) for k in range(1, YS)]
 
-    to_left = send(tiles_ref.at[pl.ds(0, rt)], nbr_tiles.at[1], left)
-    to_right = send(tiles_ref.at[pl.ds(2 * rt, rt)], nbr_tiles.at[0], right)
-
-    for c in fetch_cols:
-        c.wait()
-    for i in range(3):
-        def invert(r, _, i=i):
-            found = jnp.int32(0)
-            for t in range(rt):
-                found = jnp.where(cols_s[i, 2 - i, t] == r, jnp.int32(t), found)
-            inv_s[i, r] = found
-            return 0
-
-        lax.fori_loop(0, rt, invert, 0)
-
-    fetch_tiles.wait()
-
-    def ours(r, _):
-        for i in range(3):
-            w_v[i, r, :, :LANES] = tiles_v[i * rt + r]
-        w_v[1, r, :, LANES:] = tiles_v[rt + inv_s[1, r]].T
-        return 0
-
-    lax.fori_loop(0, rt, ours, 0)
-
     def gathered(h, copies):
         for c in copies:
             c.wait_recv()
@@ -123,6 +127,13 @@
 
     gathered(0, step3a)
     gathered(1, step3b)
+
+    share = rt // cores
+    part = pl.ds(core * share, share)
+    swapped = [
+        send(tiles_v.at[pl.ds(core * share, share)], nbr_tiles.at[1, part], left),
+        send(tiles_v.at[pl.ds(2 * rt + core * share, share)], nbr_tiles.at[0, part], right),
+    ]
     fetch_desc.wait()
 
     chunk = min(512, rows)
@@ -188,17 +199,17 @@
             at = pl.ds(pl.multiple_of(r * LANES, LANES), LANES)
             from_left = jnp.dot(
                 w_v[0, r],
-                jnp.concatenate([halo_hl[0, cols_s[1, 0, r]], halo_hl[0, inv_s[0, r]]], axis=0),
+                jnp.concatenate([halo_hl[0, cols_s[0, r, me]], halo_hl[0, inv_s[0, r]]], axis=0),
                 preferred_element_type=F32,
             )
             from_own = jnp.dot(
                 w_v[1, r],
-                jnp.concatenate([own_hl[h, cols_s[1, 1, r]], own_hl[h, inv_s[1, r]]], axis=0),
+                jnp.concatenate([own_hl[h, cols_s[1, r, me]], own_hl[h, inv_s[1, r]]], axis=0),
                 preferred_element_type=F32,
             )
             from_right = jnp.dot(
                 w_v[2, r],
-                jnp.concatenate([halo_hl[1, cols_s[1, 2, r]], halo_hl[1, inv_s[2, r]]], axis=0),
+                jnp.concatenate([halo_hl[1, cols_s[2, r, me]], halo_hl[1, inv_s[2, r]]], axis=0),
                 preferred_element_type=F32,
             )
             total = (from_left[:, :LANES] * 256.0 + from_left[:, LANES:]) * low
@@ -210,30 +221,41 @@
 
         return lax.fori_loop(0, rt, one, carry)
 
-    def total_of(p, first, second):
+    def sum_start(p, partials):
         row = lax.broadcasted_iota(I32, (8, qdev), 0)
-        value = jnp.where(
-            row == 0,
-            jnp.sum(first, axis=0, keepdims=True),
-            jnp.where(row == 1, jnp.sum(second, axis=0, keepdims=True), 0.0),
-        )
-        base = 0
-        for axis in range(3):
-            mine = base + place[axis]
-            red_v[p, mine] = value
-            copies = [send(red_v.at[p, mine], red_v.at[p, mine], peer(axis, k)) for k in range(1, sizes[axis])]
-            for c in copies:
-                c.wait_recv()
-            value = red_v[p, base]
-            for k in range(1, sizes[axis]):
-                value = value + red_v[p, base + k]
-            base += sizes[axis]
-        return value[0:1], value[1:2]
+        value = jnp.zeros((8, qdev), F32)
+        for i, partial in enumerate(partials):
+            value = jnp.where(row == i, jnp.sum(partial, axis=0, keepdims=True), value)
+        red_v[p, spot] = value
+        return [send(red_v.at[p, spot], red_v.at[p, spot], t) for t in in_plane]
+
+    def added(p, first, count):
+        value = red_v[p, first]
+        for k in range(1, count):
+            value = value + red_v[p, first + k]
+        return value
+
+    def sum_middle(p, copies):
+        for c in copies:
+            c.wait_recv()
+        mine = plane + z
+        red_v[p, mine] = added(p, 0, plane)
+        return [send(red_v.at[p, mine], red_v.at[p, mine], t) for t in along_z]
+
+    def sum_end(p, copies):
+        for c in copies:
+            c.wait_recv()
+        return added(p, plane, zs)
 
     halo0 = [encode(0, h, s0_ref, most[:, h * LANES : (h + 1) * LANES]) for h in range(halves)]
 
-    for side, copy in ((1, to_left), (0, to_right)):
+    passed = []
+    for side, copy in ((1, swapped[0]), (0, swapped[1])):
         copy.wait_recv()
+        for other in others:
+            passed.append(send(nbr_tiles.at[side, part], nbr_tiles.at[side, part], other))
+    for c in passed:
+        c.wait_recv()
 
     def theirs(r, _):
         w_v[0, r, :, LANES:] = nbr_tiles[0, inv_s[0, r]].T
@@ -255,32 +277,40 @@
         curves.append(curve)
         halo1.append(encode(1, h, m0_ref, most))
 
-    rr0, curve0 = total_of(0, square0, jnp.concatenate(curves, axis=1))
+    on_way = sum_start(0, [square0, jnp.concatenate(curves, axis=1)])
+    decode(1, 0, halo1[0])
+    on_way = sum_middle(0, on_way)
+    for h in range(halves - 1):
+        if h:
+            decode(1, h, halo1[h])
+        apply(1, h, m1_ref, lambda carry, at, cut, m: carry, 0)
+    total = sum_end(0, on_way)
+    rr0, curve0 = total[0:1], total[1:2]
     alpha0 = rr0 / curve0
 
-    def residual_square(r, square):
-        at = pl.ds(pl.multiple_of(r * LANES, LANES), LANES)
-        s0 = s0_ref[at, :]
-        r1 = s0 - alpha0 * (s0 - DAMP * m0_ref[at, :])
-        return square + jnp.sum(fold(r1 * r1), axis=0)
-
-    square1 = lax.fori_loop(0, rt, residual_square, zero)
-    rr1, _ = total_of(1, square1, square1)
+    def second_use(carry, at, cut, m1):
+        s0, m0, a = s0_ref[at, cut], m0_ref[at, cut], alpha0[:, cut]
+        s1 = s0 - DAMP * m0
+        r1 = s0 - a * s1
+        image = r1 - DAMP * (m0 - a * (m0 - DAMP * m1))
+        return tuple(c + jnp.sum(fold(r1 * v), axis=0) for c, v in zip(carry, (r1, image, s1), strict=True))
+
+    def second_pass(h):
+        cut = slice(h * LANES, (h + 1) * LANES)
+
+        def one(r, carry):
+            at = pl.ds(pl.multiple_of(r * LANES, LANES), LANES)
+            return second_use(carry, at, cut, m1_ref[at, cut])
+
+        return lax.fori_loop(0, rt, one, (small, small, small))
+
+    dots = [second_pass(h) for h in range(halves - 1)]
+    decode(1, halves - 1, halo1[halves - 1])
+    dots.append(apply(1, halves - 1, m1_ref, second_use, (small, small, small)))
+    total = sum_end(1, sum_middle(1, sum_start(1, [jnp.concatenate(d, axis=1) for d in zip(*dots, strict=True)])))
+    rr1 = total[0:1]
     beta = rr1 / rr0
-
-    def second_use(curve, at, cut, m1):
-        s0, m0 = s0_ref[at, cut], m0_ref[at, cut]
-        a, b = alpha0[:, cut], beta[:, cut]
-        d1 = (s0 - a * (s0 - DAMP * m0)) + b * s0
-        image = d1 - DAMP * ((1.0 + b) * m0 - a * (m0 - DAMP * m1))
-        return curve + jnp.sum(fold(d1 * image), axis=0)
-
-    curves = []
-    for h in range(halves):
-        decode(1, h, halo1[h])
-        curves.append(apply(1, h, m1_ref, second_use, small))
-    curve = jnp.concatenate(curves, axis=1)
-    curve1, _ = total_of(2, curve, curve)
+    curve1 = total[1:2] + beta * (2.0 * total[2:3] + beta * curve0)
     alpha1 = rr1 / curve1
     row = lax.broadcasted_iota(I32, (8, qdev), 0)
     coef_ref[...] = jnp.where(row == 0, alpha0, jnp.where(row == 1, beta, alpha1))
@@ -297,18 +327,12 @@
     halves = qdev // LANES
     zs = n // (XS * YS)
     field = pltpu.VMEM((rows, qdev), F32)
-    hops = XS + YS + zs - 3
-    copies = (zs - 1 + 2 * (XS + YS - 2)) + 2 + 2 * halves * 4 + 3 * hops
+    cores = lax.axis_size("qcol")
+    copies = (zs - 1 + 2 * (XS + YS - 2)) + 2 * cores + 2 * halves * 4 + 2 * (XS * YS + zs - 2)
     s0, m0, m1, coef = pl.pallas_call(
         functools.partial(kernel, n),
         out_shape=(field, field, field, pltpu.VMEM((8, qdev), F32)),
-        in_specs=[
-            pl.BlockSpec(memory_space=pl.ANY),
-            pl.BlockSpec(memory_space=pltpu.VMEM),
-            pl.BlockSpec(memory_space=pl.ANY),
-            pl.BlockSpec(memory_space=pl.ANY),
-            pl.BlockSpec(memory_space=pltpu.SMEM),
-        ],
+        in_specs=[pl.BlockSpec(memory_space=pltpu.HBM)] * 5,
         out_specs=[pl.BlockSpec(memory_space=pltpu.VMEM)] * 4,
         scratch_shapes=[
             pltpu.VMEM((rows, width), BF16),
@@ -323,17 +347,18 @@
             pltpu.VMEM((2, halves, 2, 8, LANES), F32),
             pltpu.VMEM((halves, rt, LANES, 2 * LANES), BF16),
             pltpu.VMEM((2, rt, LANES, 2 * LANES), BF16),
-            pltpu.VMEM((3, XS + YS + zs, 8, qdev), F32),
-            pltpu.SMEM((3, 3, rt), I32),
+            pltpu.VMEM((2, XS * YS + zs, 8, qdev), F32),
+            pltpu.SMEM((3, rt, n), I32),
+            pltpu.SMEM((n,), I32),
             pltpu.SMEM((3, rt), I32),
-            pltpu.SemaphoreType.DMA((5,)),
+            pltpu.SemaphoreType.DMA((4 + halves,)),
             pltpu.SemaphoreType.DMA((copies,)),
             pltpu.SemaphoreType.DMA((copies,)),
         ],
         compiler_params=pltpu.CompilerParams(
             collective_id=0, has_side_effects=True, vmem_limit_bytes=40 * 2**20
         ),
-    )(descriptors, queries, tiles, tile_cols, part_size)
+    )(*(pltpu.with_memory_space_constraint(v, pltpu.HBM) for v in (descriptors, queries.T, tiles, jnp.transpose(tile_cols, (1, 2, 0)), part_size)))
     alpha0, beta, alpha1 = coef[0:1], coef[1:2], coef[2:3]
     r1 = s0 - alpha0 * (s0 - DAMP * m0)
     d1 = r1 + beta * s0

time: 160 us -> 107 us (0.67)
  Pallas kernels: 152 us -> 103 us
  local copies, waits for them, and re-layouts: 3.76 us -> 0 us
    pallas_call x1, Pallas kernels: 152 us -> 103 us  [body(): pl.pallas_call(functools.partial(kernel, n), out_shape=(field, field, fie...]
    unnamed x6 -> x0, local copies, waits for them, and re-layouts: 3.76 us -> none
where the time goes in v2:
time: 107 us
  Pallas kernels  103 us (96%)
  other arithmetic  3.24 us (3%)
    pallas_call x1, Pallas kernels, body(): pl.pallas_call(functools.partial(kernel, n), out_shape=(field, field, fie...  103 us
    sub x1, other arithmetic, body(): return (alpha0 * s0 + alpha1 * d1, r1 - alpha1 * image)  3.23 us

profile of v2, /device:TPU:2, one launch (start us, length us, event | category | flops | bytes accessed | tf_op | source)
XLA Modules:
  0.0 107.3 jit_solution(16246658311060197786)
XLA Ops:
  0.6 103.4 %shard_map.68 = (f32[2048,256]{1,0:T(8,128)S(1)}, f32[2048,256]{1,0:T(8,128)S(1)}, f32[2048,256]{1,0:T(8,128)S(1)}, f32[8,256]{1,0:T(8,128)S(1)}) custom-call(bf16[2048,2048]{1,0:T(8,128)(2,1)} %desc_ref.1, bf16[16,256]{1,0:T(8,128)(2,1)} %bitcast.7, bf16[48,128,128]{2,1,0:T(8,128)(2,1)} %tiles_ref.1, s32[3,16,128]{2,1,0:T(8,128)} %bitcast.6, s32[128]{0:T(128)} %size_ref.1), custom_call_target="tpu_custom_call" | custom-call | tf_op jit(solution)/shard_map/pallas_call | solution.py:332
  104.0 3.2 %multiply_subtract_fusion = (f32[2048,256]{1,0:T(8,128)}, f32[2048,256]{1,0:T(8,128)}) fusion(f32[2048,256]{1,0:T(8,128)S(1)} %get-tuple-element.8, f32[2048,256]{1,0:T(8,128)S(1)} %get-tuple-element.9, f32[2048,256]{1,0:T(8,128)S(1)} %get-tuple-element.7, f32[256]{0:T(256)S(1)} %bitcast.8, f32[256]{0:T(256)S(1)} %bitcast.9, f32[256]{0:T(256)S(1)} %bitcast.10, ...), kind=kLoop, calls=%fused_computation | loop fusion | flops 9437184 | bytes 10489856 | tf_op jit(solution)/shard_map/sub | solution.py:366
  (1 shorter events, 0.0 us)

commit v3 on v2

--- a/solution.py
+++ b/solution.py
@@ -11,6 +11,7 @@
 LANES = 128
 STEPS = 65535.0
 DAMP = 0.99
+PIECES = 8
 MESH = pl.DeviceIdType.MESH
 F32, BF16, I32 = jnp.float32, jnp.bfloat16, jnp.int32
 
@@ -74,8 +75,8 @@
     fetch_size = pltpu.make_async_copy(size_ref, size_s, local_sem.at[3])
     fetch_size.start()
     fetch_q = [
-        pltpu.make_async_copy(q_ref.at[:, h * LANES : (h + 1) * LANES], qg.at[h, z, y, x], local_sem.at[4 + h])
-        for h in range(halves)
+        pltpu.make_async_copy(q_ref.at[:, h * LANES : (h + 1) * LANES], qg.at[(h, *at, z)], local_sem.at[4 + h])
+        for h, at in ((0, (x, y)), (1, (y, x)))
     ]
     for c in fetch_q:
         c.start()
@@ -108,32 +109,39 @@
         c.wait()
     pl.semaphore_wait(barrier, len(partners))
 
-    step1 = [send(qg.at[:, z, y, x], qg.at[:, z, y, x], peer(2, k)) for k in range(1, zs)]
-    for c in step1:
+    step1 = [[send(qg.at[(h, *at, z)], qg.at[(h, *at, z)], t) for t in along_z] for h, at in ((0, (x, y)), (1, (y, x)))]
+    for c in step1[0]:
         c.wait_recv()
-    step2a = [send(qg.at[0, :, y, x], qg.at[0, :, y, x], peer(1, k)) for k in range(1, YS)]
-    step2b = [send(qg.at[1, :, y, x], qg.at[1, :, y, x], peer(0, k)) for k in range(1, XS)]
+    step2a = [send(qg.at[0, x, y], qg.at[0, x, y], peer(1, k)) for k in range(1, YS)]
+    for c in step1[1]:
+        c.wait_recv()
+    step2b = [send(qg.at[1, y, x], qg.at[1, y, x], peer(0, k)) for k in range(1, XS)]
     for c in step2a:
         c.wait_recv()
-    step3a = [send(qg.at[0, :, :, x], qg.at[0, :, :, x], peer(0, k)) for k in range(1, XS)]
+    step3a = [send(qg.at[0, x], qg.at[0, x], peer(0, k)) for k in range(1, XS)]
     for c in step2b:
         c.wait_recv()
-    step3b = [send(qg.at[1, :, y], qg.at[1, :, y], peer(1, k)) for k in range(1, YS)]
+    step3b = [send(qg.at[1, y], qg.at[1, y], peer(1, k)) for k in range(1, YS)]
 
     def gathered(h, copies):
         for c in copies:
             c.wait_recv()
-        qcat[:, h * LANES : (h + 1) * LANES] = qg[h].reshape(qcat.shape[0], LANES)
+        block = qg.shape[4]
+        for zz in range(zs):
+            for yy in range(YS):
+                for xx in range(XS):
+                    at = ((zz * YS + yy) * XS + xx) * block
+                    qcat[at : at + block, h * LANES : (h + 1) * LANES] = qg[(h, *((xx, yy) if h == 0 else (yy, xx)), zz)]
 
     gathered(0, step3a)
-    gathered(1, step3b)
-
     share = rt // cores
     part = pl.ds(core * share, share)
     swapped = [
         send(tiles_v.at[pl.ds(core * share, share)], nbr_tiles.at[1, part], left),
         send(tiles_v.at[pl.ds(2 * rt + core * share, share)], nbr_tiles.at[0, part], right),
     ]
+    gathered(1, step3b)
+
     fetch_desc.wait()
 
     chunk = min(512, rows)
@@ -173,6 +181,11 @@
             return 0
 
         lax.fori_loop(0, rt, one, 0)
+
+    def both_ways(it, h, after=()):
+        for c in after:
+            c.wait_send()
+            sent[:] = [s for s in sent if s is not c]
         copies = []
         for side, target in ((1, left), (0, right)):
             copies.append(send(scale_v.at[it, h], hscale_v.at[it, h, side], target))
@@ -191,6 +204,21 @@
 
             lax.fori_loop(0, rt, one, 0)
 
+    def apply_own(h, out_ref):
+        cut = slice(h * LANES, (h + 1) * LANES)
+
+        def one(r, _):
+            at = pl.ds(pl.multiple_of(r * LANES, LANES), LANES)
+            from_own = jnp.dot(
+                w_v[1, r],
+                jnp.concatenate([own_hl[h, cols_s[1, r, me]], own_hl[h, inv_s[1, r]]], axis=0),
+                preferred_element_type=F32,
+            )
+            out_ref[at, cut] = from_own[:, :LANES] + from_own[:, LANES:]
+            return 0
+
+        lax.fori_loop(0, rt, one, 0, unroll=4)
+
     def apply(it, h, out_ref, use, carry):
         cut = slice(h * LANES, (h + 1) * LANES)
         low, high = hscale_v[it, h, 0][:1], hscale_v[it, h, 1][:1]
@@ -200,11 +228,6 @@
             from_left = jnp.dot(
                 w_v[0, r],
                 jnp.concatenate([halo_hl[0, cols_s[0, r, me]], halo_hl[0, inv_s[0, r]]], axis=0),
-                preferred_element_type=F32,
-            )
-            from_own = jnp.dot(
-                w_v[1, r],
-                jnp.concatenate([own_hl[h, cols_s[1, r, me]], own_hl[h, inv_s[1, r]]], axis=0),
                 preferred_element_type=F32,
             )
             from_right = jnp.dot(
@@ -213,21 +236,23 @@
                 preferred_element_type=F32,
             )
             total = (from_left[:, :LANES] * 256.0 + from_left[:, LANES:]) * low
-            total = total + (from_own[:, :LANES] + from_own[:, LANES:])
+            total = total + out_ref[at, cut]
             total = total + (from_right[:, :LANES] * 256.0 + from_right[:, LANES:]) * high
             m = jnp.where(live_of(r * LANES, total.shape), 0.5 * total, 0.0)
             out_ref[at, cut] = m
             return use(carry, at, cut, m)
 
-        return lax.fori_loop(0, rt, one, carry)
+        return lax.fori_loop(0, rt, one, carry, unroll=4)
 
     def sum_start(p, partials):
-        row = lax.broadcasted_iota(I32, (8, qdev), 0)
-        value = jnp.zeros((8, qdev), F32)
+        row = lax.broadcasted_iota(I32, (8, LANES), 0)
+        value = jnp.zeros((8, LANES), F32)
         for i, partial in enumerate(partials):
-            value = jnp.where(row == i, jnp.sum(partial, axis=0, keepdims=True), value)
-        red_v[p, spot] = value
-        return [send(red_v.at[p, spot], red_v.at[p, spot], t) for t in in_plane]
+            for h in range(halves):
+                sums = jnp.sum(partial[:, h * LANES : (h + 1) * LANES], axis=0, keepdims=True)
+                value = jnp.where(row == i * halves + h, sums, value)
+        red_v[p, z] = value
+        return [send(red_v.at[p, z], red_v.at[p, z], t) for t in along_z]
 
     def added(p, first, count):
         value = red_v[p, first]
@@ -238,16 +263,23 @@
     def sum_middle(p, copies):
         for c in copies:
             c.wait_recv()
-        mine = plane + z
-        red_v[p, mine] = added(p, 0, plane)
-        return [send(red_v.at[p, mine], red_v.at[p, mine], t) for t in along_z]
-
-    def sum_end(p, copies):
+        mine = zs + spot
+        red_v[p, mine] = added(p, 0, zs)
+        return [send(red_v.at[p, mine], red_v.at[p, mine], t) for t in in_plane]
+
+    def sum_end(p, copies, count):
         for c in copies:
             c.wait_recv()
-        return added(p, plane, zs)
-
-    halo0 = [encode(0, h, s0_ref, most[:, h * LANES : (h + 1) * LANES]) for h in range(halves)]
+        total = added(p, zs, plane)
+        return [
+            jnp.concatenate([total[i * halves + h : i * halves + h + 1] for h in range(halves)], axis=1)
+            for i in range(count)
+        ]
+
+    halo0 = []
+    for h in range(halves):
+        encode(0, h, s0_ref, most[:, h * LANES : (h + 1) * LANES])
+        halo0.append(both_ways(0, h, halo0[h - 1] if h else ()))
 
     passed = []
     for side, copy in ((1, swapped[0]), (0, swapped[1])):
@@ -264,6 +296,9 @@
 
     lax.fori_loop(0, rt, theirs, 0)
 
+    for h in range(halves):
+        apply_own(h, m0_ref)
+
     def first_use(carry, at, cut, m):
         most, curve = carry
         s0 = s0_ref[at, cut]
@@ -275,17 +310,19 @@
         decode(0, h, halo0[h])
         most, curve = apply(0, h, m0_ref, first_use, (small, small))
         curves.append(curve)
-        halo1.append(encode(1, h, m0_ref, most))
-
-    on_way = sum_start(0, [square0, jnp.concatenate(curves, axis=1)])
-    decode(1, 0, halo1[0])
-    on_way = sum_middle(0, on_way)
+        last = h == halves - 1
+        if last:
+            on_way = sum_start(0, [square0, jnp.concatenate(curves, axis=1)])
+        encode(1, h, m0_ref, most)
+        if last:
+            on_way = sum_middle(0, on_way)
+        halo1.append(both_ways(1, h, halo1[h - 1] if h else halo0[-1]))
+        apply_own(h, m1_ref)
+
     for h in range(halves - 1):
-        if h:
-            decode(1, h, halo1[h])
+        decode(1, h, halo1[h])
         apply(1, h, m1_ref, lambda carry, at, cut, m: carry, 0)
-    total = sum_end(0, on_way)
-    rr0, curve0 = total[0:1], total[1:2]
+    rr0, curve0 = sum_end(0, on_way, 2)
     alpha0 = rr0 / curve0
 
     def second_use(carry, at, cut, m1):
@@ -307,16 +344,41 @@
     dots = [second_pass(h) for h in range(halves - 1)]
     decode(1, halves - 1, halo1[halves - 1])
     dots.append(apply(1, halves - 1, m1_ref, second_use, (small, small, small)))
-    total = sum_end(1, sum_middle(1, sum_start(1, [jnp.concatenate(d, axis=1) for d in zip(*dots, strict=True)])))
-    rr1 = total[0:1]
+    on_way = sum_start(1, [jnp.concatenate(d, axis=1) for d in zip(*dots, strict=True)])
+    rr1, curve_rr, curve_rs = sum_end(1, sum_middle(1, on_way), 3)
     beta = rr1 / rr0
-    curve1 = total[1:2] + beta * (2.0 * total[2:3] + beta * curve0)
+    curve1 = curve_rr + beta * (2.0 * curve_rs + beta * curve0)
     alpha1 = rr1 / curve1
     row = lax.broadcasted_iota(I32, (8, qdev), 0)
     coef_ref[...] = jnp.where(row == 0, alpha0, jnp.where(row == 1, beta, alpha1))
 
     for c in sent:
         c.wait_send()
+
+
+def finish(s0_ref, m0_ref, m1_ref, coef_ref, rank_ref, resid_ref, rank_v, resid_v, sem):
+    alpha0, beta, alpha1 = coef_ref[0:1], coef_ref[1:2], coef_ref[2:3]
+    size = rank_ref.shape[0] // PIECES
+    step = min(64, size)
+    copies = []
+    for p in range(PIECES):
+        def one(i, _, p=p):
+            at = pl.ds(pl.multiple_of(p * size + i * step, step), step)
+            s0, m0 = s0_ref[at, :], m0_ref[at, :]
+            r1 = s0 - alpha0 * (s0 - DAMP * m0)
+            d1 = r1 + beta * s0
+            image = d1 - DAMP * ((1.0 + beta) * m0 - alpha0 * (m0 - DAMP * m1_ref[at, :]))
+            rank_v[at, :] = alpha0 * s0 + alpha1 * d1
+            resid_v[at, :] = r1 - alpha1 * image
+            return 0
+
+        lax.fori_loop(0, size // step, one, 0)
+        at = pl.ds(p * size, size)
+        for i, (src, dst) in enumerate(((rank_v, rank_ref), (resid_v, resid_ref))):
+            copies.append(pltpu.make_async_copy(src.at[at], dst.at[at], sem.at[i, p]))
+            copies[-1].start()
+    for c in copies:
+        c.wait()
 
 
 def body(descriptors, queries, tiles, tile_cols, part_size):
@@ -328,7 +390,7 @@
     zs = n // (XS * YS)
     field = pltpu.VMEM((rows, qdev), F32)
     cores = lax.axis_size("qcol")
-    copies = (zs - 1 + 2 * (XS + YS - 2)) + 2 * cores + 2 * halves * 4 + 2 * (XS * YS + zs - 2)
+    copies = (2 * (zs - 1) + 2 * (XS + YS - 2)) + 2 * cores + 2 * halves * 4 + 2 * (XS * YS + zs - 2)
     s0, m0, m1, coef = pl.pallas_call(
         functools.partial(kernel, n),
         out_shape=(field, field, field, pltpu.VMEM((8, qdev), F32)),
@@ -339,7 +401,7 @@
             pltpu.VMEM((3 * rt, LANES, LANES), BF16),
             pltpu.VMEM((2, rt, LANES, LANES), BF16),
             pltpu.VMEM((3, rt, LANES, 2 * LANES), BF16),
-            pltpu.VMEM((halves, zs, YS, XS, block, LANES), BF16),
+            pltpu.VMEM((halves, XS, YS, zs, block, LANES), BF16),
             pltpu.VMEM((width, qdev), BF16),
             pltpu.VMEM((2, halves, rt, LANES, LANES), jnp.int16),
             pltpu.VMEM((2, halves, 2, rt, LANES, LANES), jnp.int16),
@@ -347,7 +409,7 @@
             pltpu.VMEM((2, halves, 2, 8, LANES), F32),
             pltpu.VMEM((halves, rt, LANES, 2 * LANES), BF16),
             pltpu.VMEM((2, rt, LANES, 2 * LANES), BF16),
-            pltpu.VMEM((2, XS * YS + zs, 8, qdev), F32),
+            pltpu.VMEM((2, XS * YS + zs, 8, LANES), F32),
             pltpu.SMEM((3, rt, n), I32),
             pltpu.SMEM((n,), I32),
             pltpu.SMEM((3, rt), I32),
@@ -359,11 +421,19 @@
             collective_id=0, has_side_effects=True, vmem_limit_bytes=40 * 2**20
         ),
     )(*(pltpu.with_memory_space_constraint(v, pltpu.HBM) for v in (descriptors, queries.T, tiles, jnp.transpose(tile_cols, (1, 2, 0)), part_size)))
-    alpha0, beta, alpha1 = coef[0:1], coef[1:2], coef[2:3]
-    r1 = s0 - alpha0 * (s0 - DAMP * m0)
-    d1 = r1 + beta * s0
-    image = d1 - DAMP * ((1.0 + beta) * m0 - alpha0 * (m0 - DAMP * m1))
-    return alpha0 * s0 + alpha1 * d1, r1 - alpha1 * image
+    out = jax.ShapeDtypeStruct((rows, qdev), F32)
+    return pl.pallas_call(
+        finish,
+        out_shape=(out, out),
+        in_specs=[pl.BlockSpec(memory_space=pltpu.VMEM)] * 4,
+        out_specs=[pl.BlockSpec(memory_space=pltpu.HBM)] * 2,
+        scratch_shapes=[
+            pltpu.VMEM((rows, qdev), F32),
+            pltpu.VMEM((rows, qdev), F32),
+            pltpu.SemaphoreType.DMA((2, PIECES)),
+        ],
+        compiler_params=pltpu.CompilerParams(vmem_limit_bytes=16 * 2**20),
+    )(*(pltpu.with_memory_space_constraint(v, pltpu.VMEM) for v in (s0, m0, m1, coef)))
 
 
 def solution(mesh):

time: 107 us -> 99.2 us (0.927)
  Pallas kernels: 103 us -> 98.5 us
  other arithmetic: 3.24 us -> 0 us
    pallas_call x1, Pallas kernels: 103 us -> 96.1 us  [body(): pl.pallas_call(functools.partial(kernel, n), out_shape=(field, field, fie...]
    sub x1 -> x0, other arithmetic: 3.23 us -> none  [body(): return (alpha0 * s0 + alpha1 * d1, r1 - alpha1 * image)]
    pallas_call x0 -> x1, Pallas kernels: none -> 2.41 us  [body(): pl.pallas_call(finish, out_shape=(out, out), in_specs=[pl.BlockSpec(memor...]
where the time goes in v3:
time: 99.2 us; the launch traced here: 99.1 us
  Pallas kernels  98.5 us (99%)
    pallas_call x1, Pallas kernels, body(): pl.pallas_call(functools.partial(kernel, n), out_shape=(field, field, fie...  96.1 us
    pallas_call x1, Pallas kernels, body(): pl.pallas_call(finish, out_shape=(out, out), in_specs=[pl.BlockSpec(memor...  2.41 us

profile of v3, /device:TPU:2, one launch (start us, length us, event | category | flops | bytes accessed | tf_op | source)
XLA Modules:
  0.0 99.1 jit_solution(15625542069978965424)
XLA Ops:
  0.6 96.1 %shard_map.68 = (f32[2048,256]{1,0:T(8,128)S(1)}, f32[2048,256]{1,0:T(8,128)S(1)}, f32[2048,256]{1,0:T(8,128)S(1)}, f32[8,256]{1,0:T(8,128)S(1)}) custom-call(bf16[2048,2048]{1,0:T(8,128)(2,1)} %desc_ref.1, bf16[16,256]{1,0:T(8,128)(2,1)} %bitcast.3, bf16[48,128,128]{2,1,0:T(8,128)(2,1)} %tiles_ref.1, s32[3,16,128]{2,1,0:T(8,128)} %bitcast.2, s32[128]{0:T(128)} %size_ref.1), custom_call_target="tpu_custom_call" | custom-call | tf_op jit(solution)/shard_map/pallas_call | solution.py:394
  96.7 2.4 %shard_map.69 = (f32[2048,256]{1,0:T(8,128)}, f32[2048,256]{1,0:T(8,128)}) custom-call(f32[2048,256]{1,0:T(8,128)S(1)} %get-tuple-element.6.s0_ref, f32[2048,256]{1,0:T(8,128)S(1)} %get-tuple-element.7.m0_ref, f32[2048,256]{1,0:T(8,128)S(1)} %get-tuple-element.8.m1_ref, f32[8,256]{1,0:T(8,128)S(1)} %get-tuple-element.9.coef_ref), custom_call_target="tpu_custom_call" | custom-call | tf_op jit(solution)/shard_map/pallas_call | solution.py:425

commit v4 on v3

--- a/solution.py
+++ b/solution.py
@@ -123,28 +123,30 @@
         c.wait_recv()
     step3b = [send(qg.at[1, y], qg.at[1, y], peer(1, k)) for k in range(1, YS)]
 
-    def gathered(h, copies):
+    def arrived(copies):
         for c in copies:
             c.wait_recv()
+
+    def gathered(h):
         block = qg.shape[4]
         for zz in range(zs):
             for yy in range(YS):
                 for xx in range(XS):
                     at = ((zz * YS + yy) * XS + xx) * block
-                    qcat[at : at + block, h * LANES : (h + 1) * LANES] = qg[(h, *((xx, yy) if h == 0 else (yy, xx)), zz)]
-
-    gathered(0, step3a)
+                    qcat[h, at : at + block, :] = qg[(h, *((xx, yy) if h == 0 else (yy, xx)), zz)]
+
+    arrived(step3a)
     share = rt // cores
     part = pl.ds(core * share, share)
     swapped = [
         send(tiles_v.at[pl.ds(core * share, share)], nbr_tiles.at[1, part], left),
         send(tiles_v.at[pl.ds(2 * rt + core * share, share)], nbr_tiles.at[0, part], right),
     ]
-    gathered(1, step3b)
+    gathered(0)
 
     fetch_desc.wait()
 
-    chunk = min(512, rows)
+    chunk = min(1024, rows)
 
     def fold(values):
         return values.reshape(values.shape[0] // 8, 8, values.shape[1])
@@ -152,17 +154,21 @@
     def live_of(start, shape):
         return lax.broadcasted_iota(I32, shape, 0) + start < live_count
 
-    def seed(i, carry):
-        most, square = carry
-        at = pl.ds(pl.multiple_of(i * chunk, chunk), chunk)
-        sims = jnp.dot(desc_v[at, :], qcat[...], preferred_element_type=F32)
-        pos = jnp.maximum(sims, 0.0)
-        s = jnp.where(live_of(i * chunk, sims.shape), pos * pos * pos, 0.0)
-        s0_ref[at, :] = s
-        return jnp.maximum(most, jnp.max(fold(s), axis=0)), square + jnp.sum(fold(s * s), axis=0)
-
-    zero = jnp.zeros((8, qdev), F32)
-    most, square0 = lax.fori_loop(0, rows // chunk, seed, (zero, zero))
+    small = jnp.zeros((8, LANES), F32)
+
+    def seeds(h):
+        cut = slice(h * LANES, (h + 1) * LANES)
+
+        def one(i, carry):
+            most, square = carry
+            at = pl.ds(pl.multiple_of(i * chunk, chunk), chunk)
+            sims = jnp.dot(desc_v[at, :], qcat[h], preferred_element_type=F32)
+            pos = jnp.maximum(sims, 0.0)
+            s = jnp.where(live_of(i * chunk, sims.shape), pos * pos * pos, 0.0)
+            s0_ref[at, cut] = s
+            return jnp.maximum(most, jnp.max(fold(s), axis=0)), square + jnp.sum(fold(s * s), axis=0)
+
+        return lax.fori_loop(0, rows // chunk, one, (small, small))
 
     def encode(it, h, src_ref, most):
         cut = slice(h * LANES, (h + 1) * LANES)
@@ -180,7 +186,7 @@
             own_hl[h, r, :, LANES:] = (v - hi.astype(F32)).astype(BF16)
             return 0
 
-        lax.fori_loop(0, rt, one, 0)
+        lax.fori_loop(0, rt, one, 0, unroll=4)
 
     def both_ways(it, h, after=()):
         for c in after:
@@ -202,7 +208,7 @@
                 halo_hl[side, r, :, LANES:] = lax.bitwise_and(v, 255).astype(F32).astype(BF16)
                 return 0
 
-            lax.fori_loop(0, rt, one, 0)
+            lax.fori_loop(0, rt, one, 0, unroll=4)
 
     def apply_own(h, out_ref):
         cut = slice(h * LANES, (h + 1) * LANES)
@@ -276,10 +282,15 @@
             for i in range(count)
         ]
 
-    halo0 = []
+    halo0, squares = [], []
     for h in range(halves):
-        encode(0, h, s0_ref, most[:, h * LANES : (h + 1) * LANES])
-        halo0.append(both_ways(0, h, halo0[h - 1] if h else ()))
+        if h:
+            arrived(step3b)
+            gathered(1)
+        most, square = seeds(h)
+        squares.append(square)
+        encode(0, h, s0_ref, most)
+        halo0.append(both_ways(0, h))
 
     passed = []
     for side, copy in ((1, swapped[0]), (0, swapped[1])):
@@ -304,7 +315,6 @@
         s0 = s0_ref[at, cut]
         return jnp.maximum(most, jnp.max(fold(m), axis=0)), curve + jnp.sum(fold(s0 * (s0 - DAMP * m)), axis=0)
 
-    small = jnp.zeros((8, LANES), F32)
     halo1, curves = [], []
     for h in range(halves):
         decode(0, h, halo0[h])
@@ -312,11 +322,11 @@
         curves.append(curve)
         last = h == halves - 1
         if last:
-            on_way = sum_start(0, [square0, jnp.concatenate(curves, axis=1)])
+            on_way = sum_start(0, [jnp.concatenate(v, axis=1) for v in (squares, curves)])
         encode(1, h, m0_ref, most)
         if last:
             on_way = sum_middle(0, on_way)
-        halo1.append(both_ways(1, h, halo1[h - 1] if h else halo0[-1]))
+        halo1.append(both_ways(1, h))
         apply_own(h, m1_ref)
 
     for h in range(halves - 1):
@@ -339,7 +349,7 @@
             at = pl.ds(pl.multiple_of(r * LANES, LANES), LANES)
             return second_use(carry, at, cut, m1_ref[at, cut])
 
-        return lax.fori_loop(0, rt, one, (small, small, small))
+        return lax.fori_loop(0, rt, one, (small, small, small), unroll=4)
 
     dots = [second_pass(h) for h in range(halves - 1)]
     decode(1, halves - 1, halo1[halves - 1])
@@ -402,7 +412,7 @@
             pltpu.VMEM((2, rt, LANES, LANES), BF16),
             pltpu.VMEM((3, rt, LANES, 2 * LANES), BF16),
             pltpu.VMEM((halves, XS, YS, zs, block, LANES), BF16),
-            pltpu.VMEM((width, qdev), BF16),
+            pltpu.VMEM((halves, width, LANES), BF16),
             pltpu.VMEM((2, halves, rt, LANES, LANES), jnp.int16),
             pltpu.VMEM((2, halves, 2, rt, LANES, LANES), jnp.int16),
             pltpu.VMEM((2, halves, 8, LANES), F32),

time: 99.2 us -> 97 us (0.978)
  Pallas kernels: 98.5 us -> 96.3 us
    pallas_call x1, Pallas kernels: 96.1 us -> 93.9 us  [body(): pl.pallas_call(functools.partial(kernel, n), out_shape=(field, field, fie...]
where the time goes in v4:
time: 97 us; the launch traced here: 96.9 us
  Pallas kernels  96.3 us (99%)
    pallas_call x1, Pallas kernels, body(): pl.pallas_call(functools.partial(kernel, n), out_shape=(field, field, fie...  93.9 us
    pallas_call x1, Pallas kernels, body(): pl.pallas_call(finish, out_shape=(out, out), in_specs=[pl.BlockSpec(memor...  2.41 us

profile of v4, /device:TPU:2, one launch (start us, length us, event | category | flops | bytes accessed | tf_op | source)
XLA Modules:
  0.0 96.9 jit_solution(6414457059173418553)
XLA Ops:
  0.6 93.9 %shard_map.68 = (f32[2048,256]{1,0:T(8,128)S(1)}, f32[2048,256]{1,0:T(8,128)S(1)}, f32[2048,256]{1,0:T(8,128)S(1)}, f32[8,256]{1,0:T(8,128)S(1)}) custom-call(bf16[2048,2048]{1,0:T(8,128)(2,1)} %desc_ref.1, bf16[16,256]{1,0:T(8,128)(2,1)} %bitcast.3, bf16[48,128,128]{2,1,0:T(8,128)(2,1)} %tiles_ref.1, s32[3,16,128]{2,1,0:T(8,128)} %bitcast.2, s32[128]{0:T(128)} %size_ref.1), custom_call_target="tpu_custom_call" | custom-call | tf_op jit(solution)/shard_map/pallas_call | solution.py:404
  94.5 2.4 %shard_map.69 = (f32[2048,256]{1,0:T(8,128)}, f32[2048,256]{1,0:T(8,128)}) custom-call(f32[2048,256]{1,0:T(8,128)S(1)} %get-tuple-element.6.s0_ref, f32[2048,256]{1,0:T(8,128)S(1)} %get-tuple-element.7.m0_ref, f32[2048,256]{1,0:T(8,128)S(1)} %get-tuple-element.8.m1_ref, f32[8,256]{1,0:T(8,128)S(1)} %get-tuple-element.9.coef_ref), custom_call_target="tpu_custom_call" | custom-call | tf_op jit(solution)/shard_map/pallas_call | solution.py:435

commit v5 on v4

--- a/solution.py
+++ b/solution.py
@@ -315,6 +315,12 @@
         s0 = s0_ref[at, cut]
         return jnp.maximum(most, jnp.max(fold(m), axis=0)), curve + jnp.sum(fold(s0 * (s0 - DAMP * m)), axis=0)
 
+    def drain(upto):
+        for c in sent[:upto]:
+            c.wait_send()
+        del sent[:upto]
+
+    before = len(sent)
     halo1, curves = [], []
     for h in range(halves):
         decode(0, h, halo0[h])
@@ -351,10 +357,13 @@
 
         return lax.fori_loop(0, rt, one, (small, small, small), unroll=4)
 
+    drain(before)
     dots = [second_pass(h) for h in range(halves - 1)]
     decode(1, halves - 1, halo1[halves - 1])
     dots.append(apply(1, halves - 1, m1_ref, second_use, (small, small, small)))
+    before = len(sent)
     on_way = sum_start(1, [jnp.concatenate(d, axis=1) for d in zip(*dots, strict=True)])
+    drain(before)
     rr1, curve_rr, curve_rs = sum_end(1, sum_middle(1, on_way), 3)
     beta = rr1 / rr0
     curve1 = curve_rr + beta * (2.0 * curve_rs + beta * curve0)
@@ -362,8 +371,7 @@
     row = lax.broadcasted_iota(I32, (8, qdev), 0)
     coef_ref[...] = jnp.where(row == 0, alpha0, jnp.where(row == 1, beta, alpha1))
 
-    for c in sent:
-        c.wait_send()
+    drain(len(sent))
 
 
 def finish(s0_ref, m0_ref, m1_ref, coef_ref, rank_ref, resid_ref, rank_v, resid_v, sem):

time: 97 us -> 97 us (level)
  no operation moved by 1% of the time
where the time goes in v5:
time: 97 us; the launch traced here: 96.9 us
  Pallas kernels  96.3 us (99%)
    pallas_call x1, Pallas kernels, body(): pl.pallas_call(functools.partial(kernel, n), out_shape=(field, field, fie...  93.8 us
    pallas_call x1, Pallas kernels, body(): pl.pallas_call(finish, out_shape=(out, out), in_specs=[pl.BlockSpec(memor...  2.41 us

profile of v5, /device:TPU:2, one launch (start us, length us, event | category | flops | bytes accessed | tf_op | source)
XLA Modules:
  0.0 96.9 jit_solution(1694698164632678470)
XLA Ops:
  0.6 93.8 %shard_map.68 = (f32[2048,256]{1,0:T(8,128)S(1)}, f32[2048,256]{1,0:T(8,128)S(1)}, f32[2048,256]{1,0:T(8,128)S(1)}, f32[8,256]{1,0:T(8,128)S(1)}) custom-call(bf16[2048,2048]{1,0:T(8,128)(2,1)} %desc_ref.1, bf16[16,256]{1,0:T(8,128)(2,1)} %bitcast.3, bf16[48,128,128]{2,1,0:T(8,128)(2,1)} %tiles_ref.1, s32[3,16,128]{2,1,0:T(8,128)} %bitcast.2, s32[128]{0:T(128)} %size_ref.1), custom_call_target="tpu_custom_call" | custom-call | tf_op jit(solution)/shard_map/pallas_call | solution.py:412
  94.5 2.4 %shard_map.69 = (f32[2048,256]{1,0:T(8,128)}, f32[2048,256]{1,0:T(8,128)}) custom-call(f32[2048,256]{1,0:T(8,128)S(1)} %get-tuple-element.6.s0_ref, f32[2048,256]{1,0:T(8,128)S(1)} %get-tuple-element.7.m0_ref, f32[2048,256]{1,0:T(8,128)S(1)} %get-tuple-element.8.m1_ref, f32[8,256]{1,0:T(8,128)S(1)} %get-tuple-element.9.coef_ref), custom_call_target="tpu_custom_call" | custom-call | tf_op jit(solution)/shard_map/pallas_call | solution.py:443
